TPU v7x, 128 devices: a whole 4x4x4 slice. The times are simulated.
128 devices in a mesh: depth: 4 (over y), tile: 32 (over z, x, core).
Axes of the slice: x: 4, y: 4, z: 4, core: 2. Of those that a mesh axis runs over, the one named last changes fastest.
Arguments:
- field: float32 [128, 2048, 2048], P('depth', 'tile'), may hold values from -1 to 1
- absorb_coef: float32 [2], replicated, may hold values from 0.01 to 0.04
- color_coef: float32 [3, 4], replicated, may hold values from -1 to 1
- light: float32 [3], replicated, may hold values from -1 to 1
Outputs:
- image: float32 [4, 2048, 2048], P(None, 'tile', 'depth')
All inputs are finite; a program needn't handle non-finite values.
Results may differ from a plain program's by a relative error of at most 0.0003.
Values sent between devices are 32-bit elements; how exact they have to be, the bound alone decides.
A program may use at most 192 MiB of HBM per device.

v0:
```python
import jax
import jax.numpy as jnp
from jax import lax
from jax.sharding import PartitionSpec as P


def with_halo(value, sides, width):
    for axis, dim in sides:
        peers, length = (lax.axis_size(axis), value.shape[dim])
        up = [(i, (i + 1) % peers) for i in range(peers - 1)]
        down = [(j, i) for i, j in up]
        last = lax.slice_in_dim(value, length - width, length, axis=dim)
        initial = lax.slice_in_dim(value, 0, width, axis=dim)
        before = lax.ppermute(last, axis, up)
        after = lax.ppermute(initial, axis, down)
        value = jnp.concatenate([before, value, after], axis=dim)
    return value


def slab_light(padded, absorb_coef, color_coef, light):
    center = padded[1:-1, 1:-1]
    grad_z = 0.5 * (padded[2:, 1:-1] - padded[:-2, 1:-1])
    grad_x = 0.5 * (padded[1:-1, 2:] - padded[1:-1, :-2])
    side_pad = jnp.pad(center, ((0, 0), (0, 0), (1, 1)))
    grad_y = 0.5 * (side_pad[:, :, 2:] - side_pad[:, :, :-2])
    facing = jnp.abs(light[0] * grad_z + light[1] * grad_x + light[2] * grad_y)
    shade = facing / jnp.sqrt(grad_z * grad_z + grad_x * grad_x + grad_y * grad_y + 1.0)
    sigma = absorb_coef[0] + absorb_coef[1] * center * center
    coef = color_coef[:, :, None, None, None]
    poly = coef[:, 0] + center * (coef[:, 1] + center * (coef[:, 2] + center * coef[:, 3]))
    return (sigma, shade[None] * poly)


def over_front(front, back):
    return front + (1.0 - front[3:4]) * back


def on_device(field, absorb_coef, color_coef, light):
    padded = with_halo(field, (("depth", 0), ("tile", 1)), 1)
    sigma, emitted = slab_light(padded, absorb_coef, color_coef, light)
    running = jnp.cumsum(sigma, axis=0)
    before = running - sigma
    weight = (1.0 - jnp.exp(-sigma)) * jnp.exp(-before)
    color = jnp.sum(emitted * weight[None], axis=1)
    optical = running[-1]
    partial_image = jnp.concatenate([color, (1.0 - jnp.exp(-optical))[None]], axis=0)
    pieces = lax.all_to_all(partial_image[None], "depth", split_axis=3, concat_axis=0, tiled=True)
    total = pieces[0]
    for slab in range(1, pieces.shape[0]):
        total = over_front(total, pieces[slab])
    return total


def solution(mesh):
    in_specs = (P("depth", "tile", None), P(), P(), P())
    out_specs = P(None, "tile", "depth")
    return jax.shard_map(
        on_device, mesh=mesh, in_specs=in_specs, out_specs=out_specs, check_vma=False
    )
```

profile of v0, /device:TPU:38, one launch (start us, length us, event | category | flops | bytes accessed | tf_op | source)
XLA Modules:
  0.0 191.8 jit_solution(7068921546794885464)
XLA Ops:
  0.0 1.3 fusion.18
  1.3 3.5 %collective-permute-start.1 = (f32[1,64,2048]{2,1,0:T(8,128)S(1)}, f32[1,64,2048]{2,1,0:T(8,128)S(1)}, u32[]{:S(2)}, u32[]{:S(2)}) collective-permute-start(f32[1,64,2048]{2,1,0:T(8,128)S(1)} %get-tuple-element.14), channel_id=1, source_target_pairs={{0,32},{32,64},{64,96},{1,33},{33,65},{65,97},{2,34},{34,66},{66,9... | collective-permute-start | bytes 1572872 | tf_op jit(solution)/shard_map/ppermute | solution.py:14
  4.8 1.3 collective-permute-start
  6.1 9.8 %collective-permute-done.1 = f32[1,64,2048]{2,1,0:T(8,128)S(1)} collective-permute-done((f32[1,64,2048]{2,1,0:T(8,128)S(1)}, f32[1,64,2048]{2,1,0:T(8,128)S(1)}, u32[]{:S(2)}, u32[]{:S(2)}) %collective-permute-start.1) | collective-permute-done | bytes 524320 | tf_op jit(solution)/shard_map/ppermute | solution.py:14
  16.0 0.0 copy-start.2
  16.0 0.0 copy-start.3
  16.0 0.0 copy-start.1
  16.0 7.4 %constant_dynamic-update-slice_fusion.1 = f32[34,64,2048]{2,1,0:T(8,128)S(1)} fusion(f32[34,64,2048]{2,1,0:T(8,128)S(1)} %constant_dynamic-update-slice_fusion.2, f32[32,64,2048]{2,1,0:T(8,128)} %param.4), kind=kLoop, calls=%fused_computation.37 | loop fusion | bytes 33554432
  23.5 0.0 collective-permute-done
  23.5 0.0 copy-start
  23.5 6.1 %copy-done = f32[34,64,2048]{2,1,0:T(8,128)} copy-done((f32[34,64,2048]{2,1,0:T(8,128)}, f32[34,64,2048]{2,1,0:T(8,128)S(1)}, u32[]{:S(2)}) %copy-start) | copy-done | bytes 17825816
  29.6 0.5 fusion.17
  30.1 1.9 %collective-permute-start.2 = (f32[34,1,2048]{2,1,0:T(1,128)S(1)}, f32[34,1,2048]{2,1,0:T(1,128)S(1)}, u32[]{:S(2)}, u32[]{:S(2)}) collective-permute-start(f32[34,1,2048]{2,1,0:T(1,128)S(1)} %get-tuple-element.9), channel_id=1, source_target_pairs={{1,0},{2,1},{3,2},{4,3},{5,4},{6,5},{7,6},{8,7},{9,8},{10,9},{11,1... | collective-permute-start | bytes 835592 | tf_op jit(solution)/shard_map/ppermute | solution.py:15
  32.1 2.4 %collective-permute-start.3 = (f32[34,1,2048]{2,1,0:T(1,128)S(1)}, f32[34,1,2048]{2,1,0:T(1,128)S(1)}, u32[]{:S(2)}, u32[]{:S(2)}) collective-permute-start(f32[34,1,2048]{2,1,0:T(1,128)S(1)} %get-tuple-element.10), channel_id=1, source_target_pairs={{0,1},{1,2},{2,3},{3,4},{4,5},{5,6},{6,7},{7,8},{8,9},{9,10},{10,1... | collective-permute-start | bytes 835592 | tf_op jit(solution)/shard_map/ppermute | solution.py:14
  34.5 0.0 copy-done.2
  34.5 0.7 fusion.20
  37.1 0.0 copy-done.3
  37.1 0.6 fusion.21
  37.7 0.0 copy-done.1
  37.7 0.2 slice_reduce_fusion.3
  37.9 0.0 collective-permute-done.2
  37.9 2.1 %collective-permute-done.3 = f32[34,1,2048]{2,1,0:T(1,128)S(1)} collective-permute-done((f32[34,1,2048]{2,1,0:T(1,128)S(1)}, f32[34,1,2048]{2,1,0:T(1,128)S(1)}, u32[]{:S(2)}, u32[]{:S(2)}) %collective-permute-start.3) | collective-permute-done | bytes 278560 | tf_op jit(solution)/shard_map/ppermute | solution.py:14
  39.9 68.0 %rsqrt_multiply_fusion = (f32[32,64,2048]{2,1,0:T(8,128)}, f32[32,64,2048]{2,1,0:T(8,128)}, f32[32,64,2048]{2,1,0:T(8,128)}) fusion(f32[32,64,2048]{2,1,0:T(8,128)} %param.4, f32[34,64,2048]{2,1,0:T(8,128)} %copy-done, f32[34,1,2048]{2,1,0:T(1,128)S(1)} %collective-permute-done.3, f32[34,1,2048]{2,1,0:T(1,128)S(1)} %collective-permute-done.2, ...), kind=kOutput, calls=%fused_computation.13 | output fusion | flops 272629760 | bytes 103321088 | tf_op jit(solution)/shard_map/jit(cumsum)/reduce_window_sum | solution.py:41
  107.9 1.1 fusion.9
  109.1 20.6 %multiply_reduce_fusion = f32[3,64,2048]{2,1,0:T(8,128)} fusion(f32[32,64,2048]{2,1,0:T(8,128)} %get-tuple-element.12, f32[3]{0:T(128)S(1)} %get-tuple-element.6, f32[3]{0:T(128)S(1)} %get-tuple-element.7, f32[3]{0:T(128)S(1)} %get-tuple-element.8, f32[32,64,2048]{2,1,0:T(8,128)} %param.4, f32[3]{0:T(128)S(1)} %get-tuple-element.5, ...), kind=kLoop, calls=%fused_computation | loop fusion | flops 112852992 | bytes 51904560 | tf_op jit(solution)/shard_map/reduce_sum | solution.py:44
  129.6 1.6 maximum_bitcast_fusion
  131.2 3.2 %copy.13 = f32[1,4,64,2048]{2,1,0,3:T(4,128)} copy(f32[1,4,64,2048]{3,2,1,0:T(8,128)S(1)} %maximum_bitcast_fusion) | data formatting | bytes 4194304 | tf_op jit(solution)/shard_map/broadcast_in_dim | solution.py:47
  134.4 5.5 %reshape.35 = f32[4,1,131072]{2,1,0:T(1,128)S(1)} reshape(f32[2048,1,4,64]{3,2,1,0:T(4,128)} %bitcast.39) | data formatting | bytes 4194304
  139.8 32.1 %all_to_all.15 = f32[4,1,131072]{2,1,0:T(1,128)} all-to-all(f32[4,1,131072]{2,1,0:T(1,128)S(1)} %reshape.35), channel_id=1, replica_groups=mesh['depth'=4,'tile'=32] {'depth'}, dimensions={0} | all-to-all | bytes 4194304 | tf_op jit(solution)/shard_map/all_to_all | solution.py:47
  171.9 0.5 broadcast.41
  172.5 7.7 %reduce.8 = f32[4,131072]{1,0:T(4,128)S(1)} reduce(f32[4,1,131072]{2,1,0:T(1,128)} %all_to_all.15, f32[]{:T(128)} %broadcast.41), dimensions={1}, to_apply=%all_to_all.11.reduce_sub_computation | reduce | bytes 4194308 | tf_op jit(solution)/shard_map/all_to_all | solution.py:47
  180.2 4.8 %reshape.36 = f32[2048,1,4,64]{3,2,1,0:T(4,128)} reshape(f32[4,131072]{1,0:T(4,128)S(1)} %reduce.8) | data formatting | bytes 4194304
  185.0 3.7 %copy.18 = f32[1,4,64,4,512]{4,3,2,1,0:T(4,128)S(1)} copy(f32[1,4,64,4,512]{2,1,4,3,0:T(4,128)} %bitcast.40) | data formatting | bytes 4194304 | tf_op jit(solution)/shard_map/all_to_all | solution.py:47
  188.7 1.8 fusion.19
  190.4 0.1 slice_subtract_fusion.2
  190.6 0.1 fusion.13
  190.7 0.1 fusion.11
  190.9 0.9 fusion.14
  (5 shorter events, 0.1 us)
Async XLA Ops:
  1.3 14.7 %collective-permute-start.1 = (f32[1,64,2048]{2,1,0:T(8,128)S(1)}, f32[1,64,2048]{2,1,0:T(8,128)S(1)}, u32[]{:S(2)}, u32[]{:S(2)}) collective-permute-start(f32[1,64,2048]{2,1,0:T(8,128)S(1)} %get-tuple-element.14), channel_id=1, source_target_pairs={{0,32},{32,64},{64,96},{1,33},{33,65},{65,97},{2,34},{34,66},{66,9... | collective-permute-start | bytes 1572872 | tf_op jit(solution)/shard_map/ppermute | solution.py:14
  4.8 18.7 %collective-permute-start = (f32[1,64,2048]{2,1,0:T(8,128)S(1)}, f32[1,64,2048]{2,1,0:T(8,128)S(1)}, u32[]{:S(2)}, u32[]{:S(2)}) collective-permute-start(f32[1,64,2048]{2,1,0:T(8,128)S(1)} %get-tuple-element.13), channel_id=1, source_target_pairs={{32,0},{64,32},{96,64},{33,1},{65,33},{97,65},{34,2},{66,34},{98,6... | collective-permute-start | bytes 1572872 | tf_op jit(solution)/shard_map/ppermute | solution.py:15
  16.0 18.5 %copy-start.2 = (f32[3]{0:T(128)S(1)}, f32[3]{0:T(128)}, u32[]{:S(2)}) copy-start(f32[3]{0:T(128)} %param.7) | copy-start | bytes 40
  16.0 21.1 %copy-start.3 = (f32[2]{0:T(128)S(1)}, f32[2]{0:T(128)}, u32[]{:S(2)}) copy-start(f32[2]{0:T(128)} %param.5) | copy-start | bytes 28
  16.0 21.7 %copy-start.1 = (f32[3,4]{1,0:T(4,128)S(1)}, f32[3,4]{1,0:T(4,128)}, u32[]{:S(2)}) copy-start(f32[3,4]{1,0:T(4,128)} %param.6) | copy-start | bytes 148
  23.5 6.1 %copy-start = (f32[34,64,2048]{2,1,0:T(8,128)}, f32[34,64,2048]{2,1,0:T(8,128)S(1)}, u32[]{:S(2)}) copy-start(f32[34,64,2048]{2,1,0:T(8,128)S(1)} %constant_dynamic-update-slice_fusion) | copy-start | bytes 53477380
  30.1 7.7 %collective-permute-start.2 = (f32[34,1,2048]{2,1,0:T(1,128)S(1)}, f32[34,1,2048]{2,1,0:T(1,128)S(1)}, u32[]{:S(2)}, u32[]{:S(2)}) collective-permute-start(f32[34,1,2048]{2,1,0:T(1,128)S(1)} %get-tuple-element.9), channel_id=1, source_target_pairs={{1,0},{2,1},{3,2},{4,3},{5,4},{6,5},{7,6},{8,7},{9,8},{10,9},{11,1... | collective-permute-start | bytes 835592 | tf_op jit(solution)/shard_map/ppermute | solution.py:15
  32.1 7.9 %collective-permute-start.3 = (f32[34,1,2048]{2,1,0:T(1,128)S(1)}, f32[34,1,2048]{2,1,0:T(1,128)S(1)}, u32[]{:S(2)}, u32[]{:S(2)}) collective-permute-start(f32[34,1,2048]{2,1,0:T(1,128)S(1)} %get-tuple-element.10), channel_id=1, source_target_pairs={{0,1},{1,2},{2,3},{3,4},{4,5},{5,6},{6,7},{7,8},{8,9},{9,10},{10,1... | collective-permute-start | bytes 835592 | tf_op jit(solution)/shard_map/ppermute | solution.py:14
where the time goes:
time: 192 us
  other arithmetic  100 us (52%)
  local copies, waits for them, and re-layouts  36.3 us (19%)
  blocking collectives  32.1 us (17%)
  waiting for transfers between devices  11.9 us (6%)
  starting transfers between devices  9.13 us (5%)
  between operations  2.12 us (1%)
    another operation x1, other arithmetic, on_device(): running = jnp.cumsum(sigma, axis=0)  68 us
    all_to_all x1, blocking collectives, on_device(): lax.all_to_all(partial_image[None], 'depth', split_axis=3, concat_axis=0,...  32.1 us
    unnamed x13, local copies, waits for them, and re-layouts  23.9 us
    reduce_sum x1, other arithmetic, on_device(): color = jnp.sum(emitted * weight[None], axis=1)  20.6 us
    ppermute x2, waiting for transfers between devices, with_halo(): before = lax.ppermute(last, axis, up)  11.9 us
    all_to_all x1, other arithmetic, on_device(): lax.all_to_all(partial_image[None], 'depth', split_axis=3, concat_axis=0,...  7.72 us
    ppermute x2, starting transfers between devices, with_halo(): before = lax.ppermute(last, axis, up)  5.92 us
    all_to_all x2, local copies, waits for them, and re-layouts, on_device(): lax.all_to_all(partial_image[None], 'depth', split_axis=3, concat_axis=0,...  4.17 us
  transfers between devices with their start and end apart: 4, of which 2 were waited for; matrix products, arithmetic and copies ran while one was open for 5% of the time, Pallas kernels for 0%

commit v1 on v0

--- a/solution.py
+++ b/solution.py
@@ -44,7 +44,13 @@
     color = jnp.sum(emitted * weight[None], axis=1)
     optical = running[-1]
     partial_image = jnp.concatenate([color, (1.0 - jnp.exp(-optical))[None]], axis=0)
-    pieces = lax.all_to_all(partial_image[None], "depth", split_axis=3, concat_axis=0, tiled=True)
+    q_in = partial_image[None]
+    pieces = jnp.concatenate(
+        jax.lax.all_to_all(
+            jnp.stack(jnp.split(q_in, jax.lax.axis_size("depth"), 3), 0), "depth", 0, 0
+        ),
+        0,
+    )
     total = pieces[0]
     for slab in range(1, pieces.shape[0]):
         total = over_front(total, pieces[slab])

time: 192 us -> 165 us (0.86)
  local copies, waits for them, and re-layouts: 36.3 us -> 17.1 us
  other arithmetic: 100 us -> 92.1 us
    unnamed x13 -> x10, local copies, waits for them, and re-layouts: 23.9 us -> 13.6 us
    all_to_all x1 -> x0, other arithmetic: 7.72 us -> none  [on_device(): lax.all_to_all(partial_image[None], 'depth', split_axis=3, concat_axis=0,...]
    all_to_all x2 -> x0, local copies, waits for them, and re-layouts: 4.17 us -> none  [on_device(): lax.all_to_all(partial_image[None], 'depth', split_axis=3, concat_axis=0,...]
    broadcast_in_dim x1 -> x0, local copies, waits for them, and re-layouts: 3.17 us -> none  [on_device(): partial_image[None]]
where the time goes in v1:
time: 165 us; the launch traced here: 164 us
  other arithmetic  92.1 us (56%)
  blocking collectives  32 us (19%)
  local copies, waits for them, and re-layouts  17.1 us (10%)
  waiting for transfers between devices  11.9 us (7%)
  starting transfers between devices  9.13 us (6%)
  between operations  2.1 us (1%)
    another operation x1, other arithmetic, on_device(): running = jnp.cumsum(sigma, axis=0)  68 us
    all_to_all x1, blocking collectives, on_device(): jax.lax.all_to_all(jnp.stack(jnp.split(q_in, jax.lax.axis_size('depth'),...  32 us
    reduce_sum x1, other arithmetic, on_device(): color = jnp.sum(emitted * weight[None], axis=1)  21.3 us
    unnamed x10, local copies, waits for them, and re-layouts  13.6 us
    ppermute x2, waiting for transfers between devices, with_halo(): before = lax.ppermute(last, axis, up)  11.9 us
    ppermute x2, starting transfers between devices, with_halo(): before = lax.ppermute(last, axis, up)  5.92 us
  transfers between devices with their start and end apart: 4, of which 2 were waited for; matrix products, arithmetic and copies ran while one was open for 5% of the time, Pallas kernels for 0%

profile of v1, /device:TPU:38, one launch (start us, length us, event | category | flops | bytes accessed | tf_op | source)
XLA Modules:
  0.0 164.3 jit_solution(15761900933707510122)
XLA Ops:
  0.0 1.3 fusion.20
  1.3 3.5 %collective-permute-start.1 = (f32[1,64,2048]{2,1,0:T(8,128)S(1)}, f32[1,64,2048]{2,1,0:T(8,128)S(1)}, u32[]{:S(2)}, u32[]{:S(2)}) collective-permute-start(f32[1,64,2048]{2,1,0:T(8,128)S(1)} %get-tuple-element.14), channel_id=1, source_target_pairs={{0,32},{32,64},{64,96},{1,33},{33,65},{65,97},{2,34},{34,66},{66,9... | collective-permute-start | bytes 1572872 | tf_op jit(solution)/shard_map/ppermute | solution.py:14
  4.8 1.3 collective-permute-start
  6.1 9.8 %collective-permute-done.1 = f32[1,64,2048]{2,1,0:T(8,128)S(1)} collective-permute-done((f32[1,64,2048]{2,1,0:T(8,128)S(1)}, f32[1,64,2048]{2,1,0:T(8,128)S(1)}, u32[]{:S(2)}, u32[]{:S(2)}) %collective-permute-start.1) | collective-permute-done | bytes 524320 | tf_op jit(solution)/shard_map/ppermute | solution.py:14
  16.0 0.0 copy-start.2
  16.0 0.0 copy-start.3
  16.0 0.0 copy-start.1
  16.0 7.4 %constant_dynamic-update-slice_fusion.1 = f32[34,64,2048]{2,1,0:T(8,128)S(1)} fusion(f32[34,64,2048]{2,1,0:T(8,128)S(1)} %constant_dynamic-update-slice_fusion.2, f32[32,64,2048]{2,1,0:T(8,128)} %param.4), kind=kLoop, calls=%fused_computation.43 | loop fusion | bytes 33554432
  23.5 0.0 collective-permute-done
  23.5 0.0 copy-start
  23.5 6.1 %copy-done = f32[34,64,2048]{2,1,0:T(8,128)} copy-done((f32[34,64,2048]{2,1,0:T(8,128)}, f32[34,64,2048]{2,1,0:T(8,128)S(1)}, u32[]{:S(2)}) %copy-start) | copy-done | bytes 17825816
  29.6 0.5 fusion.19
  30.1 1.9 %collective-permute-start.2 = (f32[34,1,2048]{2,1,0:T(1,128)S(1)}, f32[34,1,2048]{2,1,0:T(1,128)S(1)}, u32[]{:S(2)}, u32[]{:S(2)}) collective-permute-start(f32[34,1,2048]{2,1,0:T(1,128)S(1)} %get-tuple-element.9), channel_id=1, source_target_pairs={{1,0},{2,1},{3,2},{4,3},{5,4},{6,5},{7,6},{8,7},{9,8},{10,9},{11,1... | collective-permute-start | bytes 835592 | tf_op jit(solution)/shard_map/ppermute | solution.py:15
  32.1 2.4 %collective-permute-start.3 = (f32[34,1,2048]{2,1,0:T(1,128)S(1)}, f32[34,1,2048]{2,1,0:T(1,128)S(1)}, u32[]{:S(2)}, u32[]{:S(2)}) collective-permute-start(f32[34,1,2048]{2,1,0:T(1,128)S(1)} %get-tuple-element.10), channel_id=1, source_target_pairs={{0,1},{1,2},{2,3},{3,4},{4,5},{5,6},{6,7},{7,8},{8,9},{9,10},{10,1... | collective-permute-start | bytes 835592 | tf_op jit(solution)/shard_map/ppermute | solution.py:14
  34.5 0.0 copy-done.2
  34.5 0.7 fusion.21
  37.1 0.0 copy-done.3
  37.1 0.6 fusion.22
  37.7 0.0 copy-done.1
  37.7 0.2 slice_reduce_fusion.3
  37.9 0.0 collective-permute-done.2
  37.9 2.1 %collective-permute-done.3 = f32[34,1,2048]{2,1,0:T(1,128)S(1)} collective-permute-done((f32[34,1,2048]{2,1,0:T(1,128)S(1)}, f32[34,1,2048]{2,1,0:T(1,128)S(1)}, u32[]{:S(2)}, u32[]{:S(2)}) %collective-permute-start.3) | collective-permute-done | bytes 278560 | tf_op jit(solution)/shard_map/ppermute | solution.py:14
  39.9 68.0 %rsqrt_multiply_fusion = (f32[32,64,2048]{2,1,0:T(8,128)}, f32[32,64,2048]{2,1,0:T(8,128)}, f32[32,64,2048]{2,1,0:T(8,128)}) fusion(f32[32,64,2048]{2,1,0:T(8,128)} %param.4, f32[34,64,2048]{2,1,0:T(8,128)} %copy-done, f32[34,1,2048]{2,1,0:T(1,128)S(1)} %collective-permute-done.3, f32[34,1,2048]{2,1,0:T(1,128)S(1)} %collective-permute-done.2, ...), kind=kOutput, calls=%fused_computation.13 | output fusion | flops 272629760 | bytes 103321088 | tf_op jit(solution)/shard_map/jit(cumsum)/reduce_window_sum | solution.py:41
  107.9 1.1 fusion.15
  109.1 21.3 %multiply_reduce_fusion = f32[3,64,2048]{2,1,0:T(8,128)S(1)} fusion(f32[32,64,2048]{2,1,0:T(8,128)} %get-tuple-element.12, f32[3]{0:T(128)S(1)} %get-tuple-element.6, f32[3]{0:T(128)S(1)} %get-tuple-element.7, f32[3]{0:T(128)S(1)} %get-tuple-element.8, f32[32,64,2048]{2,1,0:T(8,128)} %param.4, f32[3]{0:T(128)S(1)} %get-tuple-element.5, ...), kind=kLoop, calls=%fused_computation | loop fusion | flops 112852992 | bytes 51904560 | tf_op jit(solution)/shard_map/reduce_sum | solution.py:44
  130.3 0.2 maximum_bitcast_fusion
  130.5 0.2 slice_bitcast_fusion.7
  130.8 0.2 pad_maximum_fusion.4
  131.0 32.0 %all_to_all.5 = f32[4,1,4,64,512]{4,3,2,1,0:T(8,128)S(1)} all-to-all(f32[4,1,4,64,512]{4,3,2,1,0:T(8,128)S(1)} %pad_maximum_fusion.4), channel_id=1, replica_groups=mesh['depth'=4,'tile'=32] {'depth'}, dimensions={0} | all-to-all | bytes 4194304 | tf_op jit(solution)/shard_map/all_to_all | solution.py:49
  163.0 0.1 fusion.13
  163.2 0.2 fusion.11
  163.4 0.9 fusion.9
  (5 shorter events, 0.1 us)
Async XLA Ops:
  1.3 14.7 %collective-permute-start.1 = (f32[1,64,2048]{2,1,0:T(8,128)S(1)}, f32[1,64,2048]{2,1,0:T(8,128)S(1)}, u32[]{:S(2)}, u32[]{:S(2)}) collective-permute-start(f32[1,64,2048]{2,1,0:T(8,128)S(1)} %get-tuple-element.14), channel_id=1, source_target_pairs={{0,32},{32,64},{64,96},{1,33},{33,65},{65,97},{2,34},{34,66},{66,9... | collective-permute-start | bytes 1572872 | tf_op jit(solution)/shard_map/ppermute | solution.py:14
  4.8 18.7 %collective-permute-start = (f32[1,64,2048]{2,1,0:T(8,128)S(1)}, f32[1,64,2048]{2,1,0:T(8,128)S(1)}, u32[]{:S(2)}, u32[]{:S(2)}) collective-permute-start(f32[1,64,2048]{2,1,0:T(8,128)S(1)} %get-tuple-element.13), channel_id=1, source_target_pairs={{32,0},{64,32},{96,64},{33,1},{65,33},{97,65},{34,2},{66,34},{98,6... | collective-permute-start | bytes 1572872 | tf_op jit(solution)/shard_map/ppermute | solution.py:15
  16.0 18.5 %copy-start.2 = (f32[3]{0:T(128)S(1)}, f32[3]{0:T(128)}, u32[]{:S(2)}) copy-start(f32[3]{0:T(128)} %param.7) | copy-start | bytes 40
  16.0 21.1 %copy-start.3 = (f32[2]{0:T(128)S(1)}, f32[2]{0:T(128)}, u32[]{:S(2)}) copy-start(f32[2]{0:T(128)} %param.5) | copy-start | bytes 28
  16.0 21.7 %copy-start.1 = (f32[3,4]{1,0:T(4,128)S(1)}, f32[3,4]{1,0:T(4,128)}, u32[]{:S(2)}) copy-start(f32[3,4]{1,0:T(4,128)} %param.6) | copy-start | bytes 148
  23.5 6.1 %copy-start = (f32[34,64,2048]{2,1,0:T(8,128)}, f32[34,64,2048]{2,1,0:T(8,128)S(1)}, u32[]{:S(2)}) copy-start(f32[34,64,2048]{2,1,0:T(8,128)S(1)} %constant_dynamic-update-slice_fusion) | copy-start | bytes 53477380
  30.1 7.7 %collective-permute-start.2 = (f32[34,1,2048]{2,1,0:T(1,128)S(1)}, f32[34,1,2048]{2,1,0:T(1,128)S(1)}, u32[]{:S(2)}, u32[]{:S(2)}) collective-permute-start(f32[34,1,2048]{2,1,0:T(1,128)S(1)} %get-tuple-element.9), channel_id=1, source_target_pairs={{1,0},{2,1},{3,2},{4,3},{5,4},{6,5},{7,6},{8,7},{9,8},{10,9},{11,1... | collective-permute-start | bytes 835592 | tf_op jit(solution)/shard_map/ppermute | solution.py:15
  32.1 7.9 %collective-permute-start.3 = (f32[34,1,2048]{2,1,0:T(1,128)S(1)}, f32[34,1,2048]{2,1,0:T(1,128)S(1)}, u32[]{:S(2)}, u32[]{:S(2)}) collective-permute-start(f32[34,1,2048]{2,1,0:T(1,128)S(1)} %get-tuple-element.10), channel_id=1, source_target_pairs={{0,1},{1,2},{2,3},{3,4},{4,5},{5,6},{6,7},{7,8},{8,9},{9,10},{10,1... | collective-permute-start | bytes 835592 | tf_op jit(solution)/shard_map/ppermute | solution.py:14
